TPU v7x, 32 devices: a whole 2x2x4 slice. The times are simulated.
32 devices in a mesh: wide: 16 (over z, y, core), narrow: 2 (over x).
Axes of the slice: x: 2, y: 2, z: 4, core: 2. Of those that a mesh axis runs over, the one named last changes fastest.
Arguments:
- inputs: bfloat16 [2, 24576, 768], P(None, ('wide', 'narrow')), may hold values from -6 to 6
- coords: float32 [2, 2, 24576], P(None, None, ('wide', 'narrow')), may hold values from 0 to 1
- neighbours: int32 [2, 40, 24576], P(None, None, ('wide', 'narrow')), may hold values from 0 to 767, as said below
- counts: int32 [2, 24576], P(None, ('wide', 'narrow')), may hold values from 1 to 40, as said below
- doc_length: int32 [2, 32], P(None, ('wide', 'narrow')), may hold values from 384 to 768, as said below
- self_one: bfloat16 [768, 768], P(('wide', 'narrow')), may hold values from -0.21875 to 0.21875
- near_one: bfloat16 [768, 768], P(('wide', 'narrow')), may hold values from -0.4375 to 0.4375
- self_two: bfloat16 [768, 768], P(('wide', 'narrow')), may hold values from -0.21875 to 0.21875
- near_two: bfloat16 [768, 768], P(('wide', 'narrow')), may hold values from -0.4375 to 0.4375
- edge_proj: float32 [2, 768], replicated, may hold values from -4 to 4
- qkv_proj: bfloat16 [768, 2304], P(('wide', 'narrow')), may hold values from -0.21875 to 0.21875
- out_proj: bfloat16 [768, 768], P(('wide', 'narrow')), may hold values from -0.875 to 0.875
- up_proj: bfloat16 [768, 3072], P(('wide', 'narrow')), may hold values from -0.21875 to 0.21875
- down_proj: bfloat16 [3072, 768], P(('wide', 'narrow')), may hold values from -0.109375 to 0.109375
- norm_gains: float32 [3, 768], replicated, may hold values from 0.5 to 1.5
- norm_shifts: float32 [3, 768], replicated, may hold values from -1.5 to 1.5
- distance_rate: float32 [12], replicated, may hold values from 0.2 to 1
- order_rate: float32 [12], replicated, may hold values from -1 to 1
- cotangent: bfloat16 [2, 24576, 768], P(None, ('wide', 'narrow')), may hold values from -6 to 6
Outputs:
- outputs: bfloat16 [2, 24576, 768], P(None, ('wide', 'narrow'))
- input_grad: float32 [2, 24576, 768], P(None, ('wide', 'narrow'))
- grad_self_one: float32 [768, 768], P(('wide', 'narrow'))
- grad_near_one: float32 [768, 768], P(('wide', 'narrow'))
- grad_self_two: float32 [768, 768], P(('wide', 'narrow'))
- grad_near_two: float32 [768, 768], P(('wide', 'narrow'))
- grad_edge: float32 [2, 768], replicated
- grad_qkv: float32 [768, 2304], P(('wide', 'narrow'))
- grad_out: float32 [768, 768], P(('wide', 'narrow'))
- grad_up: float32 [768, 3072], P(('wide', 'narrow'))
- grad_down: float32 [3072, 768], P(('wide', 'narrow'))
- grad_gains: float32 [3, 768], replicated
- grad_shifts: float32 [3, 768], replicated
- grad_distance: float32 [12], replicated
- grad_order: float32 [12], replicated
Inputs may be any that keep to these rules, and one draw needn't show every extreme that they name: A token's neighbours are positions in its own row of 768 tokens, within 64 of its own position. `counts`: slots at or beyond a token's count are padding. `doc_length`: the rest of the row after the document is padding.
All inputs are finite; a program needn't handle non-finite values.
Results may differ from a plain program's by a relative error of at most 0.015.
Values may be sent and summed in bfloat16 or wider, within the bound.
A program may use at most 256 MiB of HBM per device.

v0:
```python
import functools
import jax
import jax.numpy as jnp
from jax import lax
from jax.experimental import pallas as pl
from jax.experimental.pallas import tpu as pltpu
from jax.sharding import PartitionSpec as P

RADIUS = 128
REACH = 64
BLOCK = 128
WIDE = BLOCK + 2 * REACH
SPAN = BLOCK + 2 * RADIUS
FAR = 1e10
F32 = jnp.float32
LOW = jnp.bfloat16
VMEM = 62 * 2**20
CALLS = {"front": 0, "block": 1, "attention": 2, "graph": 3}


def dot(left, right, dims):
    return lax.dot_general(left, right, ((dims[:1], dims[1:]), ((), ())), preferred_element_type=F32)


def nn(left, right):
    return dot(left, right, (1, 0))


def nt(left, right):
    return dot(left, right, (1, 1))


def tn(left, right):
    return dot(left, right, (0, 0))


def gelu_pair(pre):
    slope = 0.7978845608028654
    square = pre * pre
    half = 0.5 + 0.5 * jnp.tanh(pre * (slope + (slope * 0.044715) * square))
    act = pre * half
    deriv = half + act * (1.0 - half) * (2.0 * slope + (6.0 * slope * 0.044715) * square)
    return act, deriv


def norm_parts(values):
    centre = values - jnp.mean(values, axis=-1, keepdims=True)
    rstd = lax.rsqrt(jnp.mean(centre * centre, axis=-1, keepdims=True) + 1e-05)
    return centre * rstd, rstd


def norm_back(grad, unit, rstd, gain):
    scaled = grad * gain
    mean = jnp.mean(scaled, axis=-1, keepdims=True)
    along = jnp.mean(scaled * unit, axis=-1, keepdims=True)
    return rstd * (scaled - mean - unit * along)


def fold(values):
    rows, cols = values.shape
    return jnp.sum(values.reshape(rows // 8, 8, cols), axis=0)


def whole(shape, space=None):
    return pl.BlockSpec(shape, lambda *_: (0,) * len(shape), pipeline_mode=pl.Buffered(1))


def params(grid_rank, **more):
    return pltpu.CompilerParams(
        vmem_limit_bytes=VMEM, dimension_semantics=("arbitrary",) * grid_rank, **more
    )


def fill_bias(length, point_ref, far_ref, order_ref, row):
    tokens = point_ref.shape[2]
    side = jnp.zeros((2, RADIUS), F32)
    padded = jnp.concatenate([side, point_ref[row], side], axis=1)
    tall = jnp.concatenate([padded, jnp.zeros((6, tokens + 2 * RADIUS), F32)], axis=0)
    for b in range(tokens // BLOCK):
        window = tall[:, b * BLOCK : b * BLOCK + SPAN].T
        key_x, key_y = window[:, 0:1], window[:, 1:2]
        lanes = slice(b * BLOCK, (b + 1) * BLOCK)
        delta_x = key_x - point_ref[row, 0:1, lanes]
        delta_y = key_y - point_ref[row, 1:2, lanes]
        dist = jnp.log(1.0 + 16.0 * (delta_x * delta_x + delta_y * delta_y))
        query = lax.broadcasted_iota(jnp.int32, (SPAN, BLOCK), 1) + b * BLOCK
        key = lax.broadcasted_iota(jnp.int32, (SPAN, BLOCK), 0) + (b * BLOCK - RADIUS)
        allowed = (jnp.abs(query - key) <= RADIUS) & ((query >= length) == (key >= length))
        allowed = allowed & (key >= 0) & (key < tokens)
        far_ref[row, b] = jnp.where(allowed, dist, FAR)
        order_ref[row, b] = jnp.tanh(4.0 * delta_x)


def pair_rows(values):
    lane = lax.broadcasted_iota(jnp.int32, values.shape, 1)
    zero = jnp.zeros_like(values)
    first = jnp.where(lane < BLOCK // 2, values, zero)
    second = jnp.where(lane < BLOCK // 2, zero, values)
    return jnp.concatenate([first, second], axis=0)


def pair_pick(values):
    lane = lax.broadcasted_iota(jnp.int32, (BLOCK, BLOCK), 1)
    return jnp.where(lane < BLOCK // 2, values[:BLOCK], values[BLOCK:])


def pad_rows(pad_ref, values):
    tokens = values.shape[0]
    zeros = jnp.zeros((RADIUS, values.shape[1]), pad_ref.dtype)
    pad_ref[pl.ds(0, RADIUS), :] = zeros
    pad_ref[pl.ds(RADIUS + tokens, RADIUS), :] = zeros
    pad_ref[pl.ds(RADIUS, tokens), :] = values


FIRST, OWN, PASSED, SIBLING = 0, 1, 2, 3


class Place:
    def __init__(self, depth):
        self.depth = depth
        wide, self.x = lax.axis_index("wide"), lax.axis_index("narrow")
        self.core = lax.rem(wide, 2)
        self.y = lax.rem(lax.div(wide, 2), 2)
        self.z = lax.div(wide, 4)
        core, y, x = self.core, self.y, self.x
        self.first_y = (1 - core) * (1 - y) + core * y
        self.first_x = core * (1 - x) + (1 - core) * x
        self.second_y = core * (1 - y) + (1 - core) * y
        self.second_x = (1 - core) * (1 - x) + core * x

    def at(self, z, y, core, x):
        return ((z * 2 + y) * 2 + core, x)

    def along(self, k):
        return lax.rem(self.z + k, self.depth)

    def partners(self):
        along = [self.at(self.along(k), self.y, self.core, self.x) for k in range(1, self.depth)]
        return along + [
            self.at(self.z, self.first_y, self.core, self.first_x),
            self.at(self.z, self.second_y, self.core, self.second_x),
            self.at(self.z, self.y, 1 - self.core, self.x),
        ]


def meet(place):
    barrier = pltpu.get_barrier_semaphore()
    partners = place.partners()
    for partner in partners:
        pl.semaphore_signal(barrier, inc=1, device_id=partner, device_id_type=pl.DeviceIdType.MESH)
    pl.semaphore_wait(barrier, len(partners))


class Gather:
    def __init__(self, place, land, send, recv, group):
        self.place, self.land, self.send, self.recv, self.group = place, land, send, recv, group

    def copy(self, view, slot, device):
        return pltpu.make_async_remote_copy(
            src_ref=view, dst_ref=view, send_sem=self.send.at[self.group, slot], recv_sem=self.recv.at[self.group, slot],
            device_id=device, device_id_type=pl.DeviceIdType.MESH,
        )

    def pieces(self, stage):
        p, land = self.place, self.land
        base = p.depth - 1
        mine = land.at[:, p.y, p.core, p.x]
        if stage == "along":
            here = land.at[p.z, p.y, p.core, p.x]
            found = []
            for k in range(1, p.depth):
                there = land.at[p.along(p.depth - k), p.y, p.core, p.x]
                found.append((here, there, k - 1, p.at(p.along(k), p.y, p.core, p.x)))
            return found
        first = p.at(p.z, p.first_y, p.core, p.first_x)
        second = p.at(p.z, p.second_y, p.core, p.second_x)
        if stage == FIRST:
            return [(mine, land.at[:, p.first_y, p.core, p.first_x], base, first)]
        if stage == OWN:
            return [(mine, land.at[:, p.second_y, p.core, p.second_x], base + 1, second)]
        if stage == PASSED:
            return [(land.at[:, p.first_y, p.core, p.first_x], land.at[:, 1 - p.y, p.core, 1 - p.x], base + 2, second)]
        return [(land.at[:, :, p.core], land.at[:, :, 1 - p.core], base + 3, p.at(p.z, p.y, 1 - p.core, p.x))]

    def start(self, *stages):
        for stage in stages:
            for leaves, _, slot, device in self.pieces(stage):
                self.copy(leaves, slot, device).start()

    def arrive(self, *stages):
        for stage in stages:
            for _, arrives, slot, device in self.pieces(stage):
                self.copy(arrives, slot, device).wait_recv()

    def sent(self, *stages):
        for stage in stages or ("along", FIRST, OWN, PASSED, SIBLING):
            for leaves, _, slot, device in self.pieces(stage):
                self.copy(leaves, slot, device).wait_send()


def merge_rows(full, land):
    depth, rows = land.shape[0], land.shape[4]

    @pl.loop(0, depth * 4)
    def _(k):
        z, y, core = lax.div(k, 4), lax.rem(lax.div(k, 2), 2), lax.rem(k, 2)
        pair = jnp.concatenate([land[z, y, core, 0].astype(F32), land[z, y, core, 1].astype(F32)], axis=0)
        full[pl.ds(pl.multiple_of(k * 2 * rows, 16), 2 * rows), :] = pair.astype(LOW)


def front_kernel(remote, *refs):
    (length_ref, dist_rate_ref, order_rate_ref, near_ref, count_ref, point_ref, x_ref, edge_w_ref, gain_ref, shift_ref,
     self1_ref, near1_ref, self2_ref, near2_ref, qkv_w_ref) = refs[:15]
    refs = refs[15:]
    shards, refs = (refs[:3], refs[3:]) if remote else ((), refs)
    outs, refs = refs[:18], refs[18:]
    fulls, refs = (refs[:3], refs[3:]) if remote else ((), refs)
    (adj, cols, agg1, slope, hidden, agg2, unit, rstd, normed, low, qkv, att, probs, far, order,
     first_w, second_w, third_w, pad, point_pad, rel, keys, values, out_sem, probs_sem, in_sem) = refs[:26]
    rows, slots, tokens = near_ref.shape
    width = x_ref.shape[2]
    pairs = width // BLOCK
    blocks = tokens // BLOCK
    chunk = 2 * BLOCK

    writes = {}

    def write(k, source, dest=None):
        writes[k] = pltpu.make_async_copy(source, outs[k] if dest is None else dest, out_sem.at[k])
        writes[k].start()

    if remote:
        land_a, land_b, land_q, send, recv = refs[26:]
        place = Place(land_a.shape[0])
        lands = (land_a, land_b, land_q) + tuple(fulls)
        groups = [Gather(place, land, send, recv, g) for g, land in enumerate(lands)]
        ga, gb, gq, go, gu, gd = groups
        column = lambda land, k: land.at[place.z, place.y, place.core, place.x, :, pl.ds(k * width, width)]
        own = lambda land: land.at[place.z, place.y, place.core, place.x]
        loads = [
            [pltpu.make_async_copy(ref, column(land_a, k), in_sem.at[k]) for k, ref in enumerate((self1_ref, near1_ref))],
            [pltpu.make_async_copy(ref, column(land_b, k), in_sem.at[2 + k]) for k, ref in enumerate((self2_ref, near2_ref))],
            [pltpu.make_async_copy(qkv_w_ref, own(land_q), in_sem.at[4])],
        ] + [[pltpu.make_async_copy(ref, own(full), in_sem.at[5 + k])] for k, (ref, full) in enumerate(zip(shards, fulls))]
        for load in loads:
            for copy in load:
                copy.start()
        meet(place)

        def begin(g):
            for copy in loads[g]:
                copy.wait()
            groups[g].start("along")

        begin(0)
    else:
        loads = [
            pltpu.make_async_copy(ref, dest, in_sem.at[k])
            for k, (ref, dest) in enumerate((
                (self1_ref, first_w.at[:, pl.ds(0, width)]), (near1_ref, first_w.at[:, pl.ds(width, width)]),
                (self2_ref, second_w.at[:, pl.ds(0, width)]), (near2_ref, second_w.at[:, pl.ds(width, width)]),
                (qkv_w_ref, third_w),
            ))
        ]
        for copy in loads:
            copy.start()

    side = jnp.zeros((REACH, width), LOW)
    pad[pl.ds(0, REACH), :] = side
    pad[pl.ds(tokens + REACH, REACH), :] = side

    @pl.loop(0, rows)
    def _(row):
        length = length_ref[row]
        pad[pl.ds(REACH, tokens), :] = x_ref[row]
        points = point_ref[row]
        high = points.astype(LOW).astype(F32)
        mid = (points - high).astype(LOW).astype(F32)
        tail = points - high - mid
        split = jnp.concatenate([high, mid, tail, jnp.ones((1, tokens), F32), jnp.zeros((9, tokens), F32)], axis=0)
        edge_side = jnp.zeros((16, REACH), F32)
        point_pad[...] = jnp.concatenate([edge_side, split, edge_side], axis=1).astype(LOW)

        @pl.loop(0, blocks)
        def _(b):
            start = pl.multiple_of(b * BLOCK, BLOCK)
            lanes = pl.ds(start, BLOCK)
            near = near_ref[row, :, lanes]
            count = count_ref[row, :, lanes]
            spot = lax.broadcasted_iota(jnp.int32, (1, BLOCK), 1) + start
            slot = lax.broadcasted_iota(jnp.int32, (slots, BLOCK), 0)
            same = (near >= length) == (spot >= length)
            rel[...] = jnp.where((slot < count) & same, near - (start - REACH), -1)
            target = lax.broadcasted_iota(jnp.int32, (WIDE, BLOCK), 0)
            total = jnp.zeros((WIDE, BLOCK), F32)
            for s in range(slots):
                total = total + jnp.where(rel[s : s + 1, :] == target, 1.0, 0.0)
            band = total.astype(LOW)
            adj[row, b] = band
            sums = nn(point_pad[:, pl.ds(start, WIDE)], band)
            inverse = 1.0 / count.astype(F32)
            here = point_ref[row, :, lanes]
            edge = (sums[0:2] + sums[2:4] + sums[4:6] - sums[6:7] * here) * inverse
            lines = jnp.concatenate([edge, inverse, jnp.zeros((5, BLOCK), F32)], axis=0).T
            cols[row, lanes, :] = lines
            agg = tn(band, pad[pl.ds(start, WIDE), :])
            agg1[row, lanes, :] = (agg * lines[:, 2:3]).astype(LOW)

        if remote:
            @pl.when(row == 0)
            def _():
                ga.arrive("along")
                ga.start(FIRST, OWN)
                begin(1)

    write(0, adj)
    write(1, cols)
    write(2, agg1)
    if remote:
        ga.arrive(FIRST)
        ga.start(PASSED)
        gb.arrive("along")
        gb.start(FIRST, OWN)
        begin(2)

    @pl.loop(0, rows)
    def _(row):
        fill_bias(length_ref[row], point_ref, far, order, row)

    write(13, far)
    write(14, order)
    if remote:
        ga.arrive(OWN, PASSED)
        ga.start(SIBLING)
        gb.arrive(FIRST)
        gb.start(PASSED)
        ga.arrive(SIBLING)
        merge_rows(first_w, land_a)
    else:
        for copy in loads:
            copy.wait()
        write(16, second_w)
        write(17, third_w)
    write(15, first_w)

    @pl.loop(0, rows)
    def _(row):
        for c in range(tokens // chunk):
            part = slice(c * chunk, (c + 1) * chunk)
            pre = nn(x_ref[row, part, :], first_w[:, 0:width])
            pre = pre + nn(agg1[row, part, :], first_w[:, width : 2 * width])
            pre = pre + cols[row, part, 0:1] * edge_w_ref[0:1, :] + cols[row, part, 1:2] * edge_w_ref[1:2, :]
            act, deriv = gelu_pair(pre)
            slope[row, part, :] = deriv.astype(LOW)
            hidden[row, part, :] = act.astype(LOW)
            pad[REACH + c * chunk : REACH + (c + 1) * chunk, :] = act.astype(LOW)
        for b in range(blocks):
            lanes = slice(b * BLOCK, (b + 1) * BLOCK)
            agg = tn(adj[row, b], pad[b * BLOCK : b * BLOCK + WIDE, :])
            agg2[row, lanes, :] = (agg * cols[row, lanes, 2:3]).astype(LOW)
        if remote:
            @pl.when(row == 0)
            def _():
                gb.arrive(OWN, PASSED)
                gb.start(SIBLING)
                gq.arrive("along")
                gq.start(FIRST, OWN)
                begin(3)
                begin(4)

    write(3, slope)
    write(4, hidden)
    write(5, agg2)
    if remote:
        gb.arrive(SIBLING)
        merge_rows(second_w, land_b)
        write(16, second_w)

    @pl.loop(0, rows)
    def _(row):
        for c in range(tokens // chunk):
            part = slice(c * chunk, (c + 1) * chunk)
            resid = x_ref[row, part, :].astype(F32) + nn(hidden[row, part, :], second_w[:, 0:width])
            resid = resid + nn(agg2[row, part, :], second_w[:, width : 2 * width])
            plain, scale = norm_parts(resid)
            unit[row, part, :] = plain.astype(LOW)
            rstd[row, part, :] = scale
            out = plain * gain_ref[0:1, :] + shift_ref[0:1, :]
            normed[row, part, :] = out
            low[row, part, :] = out.astype(LOW)
        if remote:
            @pl.when(row == 0)
            def _():
                gq.arrive(FIRST)
                gq.start(PASSED)
                for g in (go, gu):
                    g.arrive("along")
                    g.start(FIRST, OWN)
                begin(5)

    write(6, unit)
    write(7, rstd)
    write(8, normed)
    write(9, low)
    if remote:
        gq.arrive(OWN, PASSED)
        gq.start(SIBLING)
        gq.arrive(SIBLING)
        merge_rows(third_w, land_q)
        write(17, third_w)

    @pl.loop(0, rows)
    def _(row):
        for c in range(tokens // chunk):
            part = slice(c * chunk, (c + 1) * chunk)
            out = nn(low[row, part, :], third_w[...]).astype(LOW)
            for k in range(3 * pairs):
                qkv[k, row, part, :] = out[:, k * BLOCK : (k + 1) * BLOCK]

    write(10, qkv)
    zeros = jnp.zeros((RADIUS, BLOCK), LOW)
    for ref in (keys, values):
        ref[pl.ds(0, RADIUS), :] = zeros
        ref[pl.ds(RADIUS + tokens, RADIUS), :] = zeros

    @pl.loop(0, rows * pairs)
    def _(turn):
        row, pair, slot = lax.div(turn, pairs), lax.rem(turn, pairs), lax.rem(turn, 2)
        if remote:
            @pl.when(turn == 1)
            def _():
                for g in (go, gu):
                    g.arrive(FIRST)
                    g.start(PASSED)
                gd.arrive("along")
                gd.start(FIRST, OWN)

            @pl.when(turn == 6)
            def _():
                for g in (go, gu):
                    g.arrive(OWN, PASSED)
                    g.start(SIBLING)

        def probs_copy(t, s):
            return pltpu.make_async_copy(
                probs.at[s], outs[12].at[lax.div(t, pairs), lax.rem(t, pairs)], probs_sem.at[s]
            )

        @pl.when(turn >= 2)
        def _():
            probs_copy(turn - 2, slot).wait()

        keys[pl.ds(RADIUS, tokens), :] = qkv[pairs + pair, row]
        values[pl.ds(RADIUS, tokens), :] = qkv[2 * pairs + pair, row]
        for b in range(blocks):
            lanes = slice(b * BLOCK, (b + 1) * BLOCK)
            window = slice(b * BLOCK, b * BLOCK + SPAN)
            queries = pair_rows(qkv[pair, row, lanes, :] * 0.125)
            raw = nt(keys[window, :], queries)
            sides = []
            for h in range(2):
                bias = order_rate_ref[2 * pair + h] * order[row, b] - dist_rate_ref[2 * pair + h] * far[row, b]
                scores = raw[:, h * BLOCK : (h + 1) * BLOCK] + bias
                grown = jnp.exp(scores - jnp.max(scores, axis=0, keepdims=True))
                scale = 1.0 / jnp.sum(grown, axis=0, keepdims=True)
                sides.append((grown * scale).astype(LOW))
            both = jnp.concatenate(sides, axis=1)
            probs[slot, b] = both
            att[pair, row, lanes, :] = pair_pick(tn(both, values[window, :])).astype(LOW)
        probs_copy(turn, slot).start()

    last = rows * pairs
    for turn in (last - 2, last - 1):
        pltpu.make_async_copy(probs.at[turn % 2], outs[12].at[turn // pairs, turn % pairs], probs_sem.at[turn % 2]).wait()
    write(11, att)
    if remote:
        for g in (go, gu):
            g.arrive(SIBLING)
        gd.arrive(FIRST, OWN)
        for g in groups[:5]:
            g.sent()
        gd.sent("along", FIRST, OWN)
    for copy in writes.values():
        copy.wait()


def front(remote, depth, length, dist_rate, order_rate, near, count, point, x, edge_w, gains, shifts, weights, shards):
    rows, tokens, width = x.shape
    slots = near.shape[1]
    blocks, pairs = tokens // BLOCK, width // BLOCK
    smem, vmem, hbm = (pl.BlockSpec(memory_space=s) for s in (pltpu.SMEM, pltpu.VMEM, pl.ANY))
    each = lambda dtype, *shape: ((rows,) + shape, dtype)
    kept = [
        each(LOW, blocks, WIDE, BLOCK),
        each(F32, tokens, 8),
        each(LOW, tokens, width),
        each(LOW, tokens, width),
        each(LOW, tokens, width),
        each(LOW, tokens, width),
        each(LOW, tokens, width),
        each(F32, tokens, 1),
        each(F32, tokens, width),
        each(LOW, tokens, width),
        ((3 * pairs, rows, tokens, BLOCK), LOW),
        ((pairs, rows, tokens, BLOCK), LOW),
        each(LOW, pairs, blocks, SPAN, 2 * BLOCK),
        each(F32, blocks, SPAN, BLOCK),
        each(F32, blocks, SPAN, BLOCK),
        ((width, 2 * width), LOW),
        ((width, 2 * width), LOW),
        ((width, 3 * width), LOW),
    ]
    out_shape = [jax.ShapeDtypeStruct(*k) for k in kept]
    kept[12] = ((2, blocks, SPAN, 2 * BLOCK), LOW)
    scratch = [pltpu.VMEM(*k) for k in kept]
    scratch += [
        pltpu.VMEM((tokens + 2 * REACH, width), LOW),
        pltpu.VMEM((16, tokens + 2 * REACH), LOW),
        pltpu.VMEM((slots, BLOCK), jnp.int32),
        pltpu.VMEM((tokens + 2 * RADIUS, BLOCK), LOW),
        pltpu.VMEM((tokens + 2 * RADIUS, BLOCK), LOW),
        pltpu.SemaphoreType.DMA((18,)),
        pltpu.SemaphoreType.DMA((2,)),
        pltpu.SemaphoreType.DMA((8,)),
    ]
    more = {}
    if remote:
        blocked = lambda shape: (depth, 2, 2, 2) + shape
        out_shape += [jax.ShapeDtypeStruct(blocked(s.shape), LOW) for s in shards]
        share = weights[0].shape[0]
        scratch += [pltpu.VMEM(blocked((share, k * width)), LOW) for k in (2, 2, 3)]
        scratch += [pltpu.SemaphoreType.DMA((6, depth + 3))] * 2
        more = {"collective_id": CALLS["front"], "has_side_effects": True}
    return pl.pallas_call(
        functools.partial(front_kernel, remote),
        in_specs=[smem] * 3 + [vmem] * 7 + [hbm] * (len(weights) + len(shards)),
        out_specs=[hbm] * len(out_shape),
        out_shape=out_shape,
        scratch_shapes=scratch,
        compiler_params=pltpu.CompilerParams(vmem_limit_bytes=VMEM, **more),
        name="front",
    )(length, dist_rate, order_rate, near, count, point, x, edge_w, gains, shifts, *weights, *shards)


TILE = 512


def block_kernel(remote, steps, *refs):
    (att_ref, normed_in, cot_ref, out_w_ref, up_ref, down_in, gain_ref, shift_ref,
     result_ref, two_out, grad_att_ref, grad_out_out, grad_up_ref, grad_down_ref, norms_ref,
     act_all, up_all, second_all, down_all, attn_all, normed_all, unit_all, rstd_all, down_w, in_sem, out_sem) = refs[:26]
    step = pl.program_id(0)
    turns, tokens, half = act_all.shape
    parts, piece = turns // 2, 2 * half
    width = normed_all.shape[1]
    load = pltpu.make_async_copy(normed_in, normed_all, in_sem.at[0])
    write_two = pltpu.make_async_copy(normed_all, two_out, out_sem.at[0])
    write_out = pltpu.make_async_copy(unit_all.at[pl.ds(0, width)], grad_out_out, out_sem.at[1])

    if remote:
        send, recv = refs[26:]
        place = Place(parts)
        mine, first, second, last = [
            down_w.at[:, y, place.core, x]
            for y, x in (
                (place.y, place.x), (place.first_y, place.first_x), (place.second_y, place.second_x), (1 - place.y, 1 - place.x)
            )
        ]
        loads = [
            pltpu.make_async_copy(down_in.at[:, y, place.core, x], view, in_sem.at[1 + k])
            for k, (y, x, view) in enumerate((
                (place.y, place.x, mine), (place.first_y, place.first_x, first), (place.second_y, place.second_x, second)
            ))
        ]

        def copy(view, slot, device):
            return pltpu.make_async_remote_copy(
                src_ref=view, dst_ref=view, send_sem=send.at[slot], recv_sem=recv.at[slot],
                device_id=device, device_id_type=pl.DeviceIdType.MESH,
            )

        partner = place.at(place.z, place.second_y, place.core, place.second_x)
        sibling = place.at(place.z, place.y, 1 - place.core, place.x)
        pass_on, arriving = copy(first, 4, partner), copy(last, 4, partner)
        across = [copy(view, k, sibling) for k, view in enumerate((mine, first, second, last))]
        theirs = [
            copy(down_w.at[:, y, 1 - place.core, x], k, sibling)
            for k, (y, x) in enumerate((
                (place.y, place.x), (place.second_y, place.second_x), (place.first_y, place.first_x), (1 - place.y, 1 - place.x)
            ))
        ]

        def begin():
            for item in loads:
                item.start()
            meet(place)
            loads[1].wait()
            pass_on.start()
            across[1].start()
            loads[0].wait()
            across[0].start()
            loads[2].wait()
            across[2].start()

        def finish():
            arriving.wait_recv()
            across[3].start()
            for item in theirs:
                item.wait_recv()
            for item in across:
                item.wait_send()
            pass_on.wait_send()
    else:
        full = pltpu.make_async_copy(down_in, down_w, in_sem.at[1])
        begin, finish = full.start, full.wait

    def put(ref, c, at, value):
        ref[2 * c, at, :], ref[2 * c + 1, at, :] = value[:, :half], value[:, half:]

    def get(ref, c, at):
        return jnp.concatenate([ref[2 * c, at, :], ref[2 * c + 1, at, :]], axis=1)

    def down_rows(c):
        return down_w[c].reshape(piece, width)

    @pl.when(step == 0)
    def _():
        load.start()
        norms_ref[...] = jnp.zeros_like(norms_ref)
        begin()
        load.wait()

    @pl.when(step < steps)
    def _():
        at = pl.ds(pl.multiple_of(step * TILE, TILE), TILE)
        att = jnp.concatenate([att_ref[k, at, :] for k in range(att_ref.shape[0])], axis=1)
        unit, rstd = norm_parts(normed_all[at, :] + nn(att, out_w_ref[...]))
        unit_all[at, :] = unit.astype(LOW)
        rstd_all[at, :] = rstd
        normed = unit * gain_ref[1:2, :] + shift_ref[1:2, :]
        normed_all[at, :] = normed
        second_all[at, :] = normed.astype(LOW)
        for c in range(parts):
            act, deriv = gelu_pair(nn(second_all[at, :], up_ref[:, c * piece : (c + 1) * piece]))
            put(act_all, c, at, act.astype(LOW))
            put(up_all, c, at, deriv.astype(LOW))

    @pl.when(step == steps)
    def _():
        finish()

    @pl.when((step >= steps) & (step < 2 * steps))
    def _():
        at = pl.ds(pl.multiple_of((step - steps) * TILE, TILE), TILE)
        resid = normed_all[at, :]
        for c in range(parts):
            resid = resid + nn(get(act_all, c, at), down_rows(c))
        unit, rstd = norm_parts(resid)
        result_ref[...] = (unit * gain_ref[2:3, :] + shift_ref[2:3, :]).astype(LOW)
        cot = cot_ref[...].astype(F32)
        norms_ref[2] += fold(cot * unit)
        norms_ref[3] += fold(cot)
        grad = norm_back(cot, unit, rstd, gain_ref[2:3, :])
        down_all[at, :] = grad.astype(LOW)
        for c in range(parts):
            up_low = (nt(down_all[at, :], down_rows(c)) * get(up_all, c, at).astype(F32)).astype(LOW)
            put(up_all, c, at, up_low)
            grad = grad + nt(up_low, up_ref[:, c * piece : (c + 1) * piece])
        unit = unit_all[at, :].astype(F32)
        norms_ref[0] += fold(grad * unit)
        norms_ref[1] += fold(grad)
        grad = norm_back(grad, unit, rstd_all[at, :], gain_ref[1:2, :])
        normed_all[at, :] = grad
        low = grad.astype(LOW)
        attn_all[at, :] = low
        grad_att_ref[...] = nt(low, out_w_ref[...]).astype(LOW)

    @pl.when(step == 2 * steps)
    def _():
        write_two.start()
        att = jnp.concatenate([att_ref[k] for k in range(att_ref.shape[0])], axis=1)
        unit_all[pl.ds(0, width), :] = tn(att, attn_all[...]).astype(LOW)
        write_out.start()

    @pl.when(step >= 2 * steps)
    def _():
        turn = step - 2 * steps
        grad_down_ref[...] = tn(act_all[turn], down_all[...]).astype(LOW)
        grad_up_ref[...] = tn(second_all[...], up_all[turn]).astype(LOW)

    @pl.when(step == 2 * steps + turns - 1)
    def _():
        write_two.wait()
        write_out.wait()


def block_both(remote, depth, att, normed, cot, out_w, up, down, gains, shifts):
    tokens, width = normed.shape
    wide = up.shape[1]
    steps = tokens // TILE
    parts = depth if remote else 4
    piece = wide // parts
    tile = pl.BlockSpec((TILE, width), lambda s: (jnp.clip(s - steps, 0, steps - 1), 0))
    late = lambda s: jnp.maximum(s - 2 * steps, 0)
    hbm = pl.BlockSpec(memory_space=pl.ANY)
    down = down if remote else down.reshape(parts, piece, width)
    more = {"collective_id": CALLS["block"], "has_side_effects": True} if remote else {}
    wide_low = pltpu.VMEM((2 * parts, tokens, piece // 2), LOW)
    tall_low = pltpu.VMEM((tokens, width), LOW)
    return pl.pallas_call(
        functools.partial(block_kernel, remote, steps),
        grid=(2 * steps + 2 * parts,),
        in_specs=[
            whole(att.shape), hbm, tile, whole((width, width)), whole(up.shape), hbm, whole(gains.shape), whole(shifts.shape),
        ],
        out_specs=[
            tile, hbm, tile, hbm,
            pl.BlockSpec((width, piece // 2), lambda s: (0, late(s))),
            pl.BlockSpec((piece // 2, width), lambda s: (late(s), 0)),
            pl.BlockSpec((4, 8, width), lambda s: (0, 0, 0)),
        ],
        out_shape=[
            jax.ShapeDtypeStruct((tokens, width), LOW),
            jax.ShapeDtypeStruct((tokens, width), F32),
            jax.ShapeDtypeStruct((tokens, width), LOW),
            jax.ShapeDtypeStruct((width, width), LOW),
            jax.ShapeDtypeStruct(up.shape, LOW),
            jax.ShapeDtypeStruct((wide, width), LOW),
            jax.ShapeDtypeStruct((4, 8, width), F32),
        ],
        scratch_shapes=[
            wide_low, wide_low, tall_low, tall_low, tall_low,
            pltpu.VMEM((tokens, width), F32),
            tall_low,
            pltpu.VMEM((tokens, 1), F32),
            pltpu.VMEM(down.shape, LOW),
            pltpu.SemaphoreType.DMA((4,)),
            pltpu.SemaphoreType.DMA((2,)),
        ]
        + ([pltpu.SemaphoreType.DMA((5,))] * 2 if remote else []),
        compiler_params=params(1, **more),
        name="block_both",
    )(att, normed, cot, out_w, up, down, gains, shifts)


class Scatter:
    def __init__(self, place, leaving, room, send, recv, group):
        self.place, self.leaving, self.send, self.recv, self.group = place, leaving, send, recv, group
        self.total, self.lands = room[0], room[1:]

    def copies(self, stage):
        p, total = self.place, self.total
        if stage == 0:
            found = [(self.leaving, self.lands[0], 0, p.at(p.z, p.y, 1 - p.core, p.x))]
        elif stage == 1:
            second = p.at(p.z, p.second_y, p.core, p.second_x)
            found = [
                (total.at[:, p.second_y, p.second_x], self.lands[1].at[0], 1, second),
                (total.at[:, 1 - p.y, 1 - p.x], self.lands[1].at[1], 2, second),
            ]
        elif stage == 2:
            first = p.at(p.z, p.first_y, p.core, p.first_x)
            found = [(total.at[:, p.first_y, p.first_x], self.lands[2], 3, first)]
        else:
            found = [
                (total.at[p.along(k), p.y, p.x], self.lands[3].at[k - 1], 3 + k, p.at(p.along(k), p.y, p.core, p.x))
                for k in range(1, p.depth)
            ]
        return [
            pltpu.make_async_remote_copy(
                src_ref=source, dst_ref=land, send_sem=self.send.at[self.group, slot],
                recv_sem=self.recv.at[self.group, slot], device_id=device, device_id_type=pl.DeviceIdType.MESH,
            )
            for source, land, slot, device in found
        ]

    def start(self, stage):
        for copy in self.copies(stage):
            copy.start()

    def arrive(self, stage):
        for copy in self.copies(stage):
            copy.wait_recv()

    def add(self, y, x, land):
        @pl.loop(0, self.place.depth)
        def _(z):
            self.total[z, y, x] = (self.total[z, y, x].astype(F32) + land(z).astype(F32)).astype(LOW)

    def fold(self, stage, go=True):
        p = self.place
        self.arrive(stage)
        if stage == 0:
            add = lambda y, x: self.add(y, x, lambda z: self.lands[0][z, y, x])
            add(p.second_y, p.second_x)
            add(1 - p.y, 1 - p.x)
            if go:
                self.start(1)
            add(p.first_y, p.first_x)
            add(p.y, p.x)
        elif stage == 1:
            self.add(p.first_y, p.first_x, lambda z: self.lands[1][1, z])
            if go:
                self.start(2)
            self.add(p.y, p.x, lambda z: self.lands[1][0, z])
        else:
            self.add(p.y, p.x, lambda z: self.lands[2][z])
            if go:
                self.start(3)

    def finish(self):
        p = self.place
        self.arrive(3)
        result = self.total[p.z, p.y, p.x].astype(F32)
        for k in range(p.depth - 1):
            result = result + self.lands[3][k].astype(F32)
        return result

    def sent(self, stages=4):
        for stage in range(stages):
            for copy in self.copies(stage):
                copy.wait_send()


class Tail:
    def __init__(self, place, parts, room, send, recv, own_sem, group):
        self.place = place
        self.total, self.land, self.far = room
        self.load = pltpu.make_async_copy(parts.at[1], self.total, own_sem.at[group])
        make = lambda source, land, slot, device: pltpu.make_async_remote_copy(
            src_ref=source, dst_ref=land, send_sem=send.at[group, slot], recv_sem=recv.at[group, slot],
            device_id=device, device_id_type=pl.DeviceIdType.MESH,
        )
        p = place
        self.across = make(parts.at[0], self.land, 0, p.at(p.z, p.first_y, p.core, p.first_x))
        self.along = [
            make(self.total.at[p.along(k)], self.far.at[k - 1], k, p.at(p.along(k), p.y, p.core, p.x))
            for k in range(1, p.depth)
        ]

    def fold(self):
        self.load.wait()
        self.across.wait_recv()

        @pl.loop(0, self.place.depth)
        def _(z):
            self.total[z] = (self.total[z].astype(F32) + self.land[z].astype(F32)).astype(LOW)

        for copy in self.along:
            copy.start()

    def finish(self):
        for copy in self.along:
            copy.wait_recv()
        result = self.total[self.place.z].astype(F32)
        for k in range(self.place.depth - 1):
            result = result + self.far[k].astype(F32)
        for copy in [self.across] + self.along:
            copy.wait_send()
        return result


def scatter_room(depth, share, cols, kept=()):
    return [
        pltpu.VMEM(shape + (share, cols), LOW)
        for shape in (kept + (depth, 2, 2), (depth, 2, 2), (2, depth), (depth,), (depth - 1,))
    ]


def attention_back_kernel(remote, pairs, *refs):
    (q_ref, k_ref, v_ref, grad_ref, probs_ref, far_ref, order_ref, low_ref) = refs[:8]
    refs = refs[8:]
    sources, refs = (refs[:3], refs[3:]) if remote else ((), refs)
    (dq_ref, dk_ref, dv_ref, rate_ref, grad_qkv_ref), refs = refs[:5], refs[5:]
    (down_ref, *parts), refs = (refs[:3], refs[3:]) if remote else ((None,), refs)
    (keys, values, grad_keys, grad_values, all_q, all_k, all_v), refs = refs[:7], refs[7:]
    step = pl.program_id(0)
    tokens = q_ref.shape[2]
    turns = all_q.shape[0] * pairs

    def when(k, action):
        @pl.when(step == k)
        def _():
            action()

    if remote:
        rooms, (send, recv, own_sem, part_sem) = [refs[5 * g : 5 * g + 5] for g in range(3)], refs[15:]
        place = Place(rooms[0][0].shape[0])
        own = [
            pltpu.make_async_copy(source.at[:, :, place.core], room[0], own_sem.at[g])
            for g, (source, room) in enumerate(zip(sources, rooms))
        ]
        groups = [
            Scatter(place, source.at[:, :, 1 - place.core], room, send, recv, g)
            for g, (source, room) in enumerate(zip(sources, rooms))
        ]
        down, out, up = groups

        def begin():
            for copy in own:
                copy.start()
            meet(place)
            down.start(0)

        def first(k, go=True):
            own[k].wait()
            groups[k].fold(0, go)

        when(0, begin)
        def second():
            down.fold(1)
            out.start(1)
            up.start(1)

        when(1, lambda: (first(0), out.start(0), up.start(0)))
        when(3, lambda: (first(1, False), first(2, False)))
        when(7, second)
        when(11, lambda: down.fold(2))

    @pl.when(step < turns)
    def _():
        row, pair = lax.div(step, pairs), lax.rem(step, pairs)
        pad_rows(keys, k_ref[0, 0])
        pad_rows(values, v_ref[0, 0])
        grad_keys[...] = jnp.zeros_like(grad_keys)
        grad_values[...] = jnp.zeros_like(grad_values)
        sums = [jnp.zeros((8, BLOCK), F32)] * 4
        cols = pl.ds(pl.multiple_of(pair * BLOCK, BLOCK), BLOCK)
        for b in range(tokens // BLOCK):
            lanes = slice(b * BLOCK, (b + 1) * BLOCK)
            window = slice(b * BLOCK, b * BLOCK + SPAN)
            queries = pair_rows(q_ref[0, 0, lanes, :] * 0.125)
            grads = pair_rows(grad_ref[0, lanes, :])
            probs_low = probs_ref[0, 0, b]
            back = nt(values[window, :], grads)
            dist = jnp.where(far_ref[0, b] < FAR, far_ref[0, b], 0.0)
            order = order_ref[0, b]
            sides = []
            for h in range(2):
                probs = probs_low[:, h * BLOCK : (h + 1) * BLOCK].astype(F32)
                part = back[:, h * BLOCK : (h + 1) * BLOCK]
                delta = jnp.sum(probs * part, axis=0, keepdims=True)
                scores = probs * (part - delta)
                sums[2 * h] = sums[2 * h] - fold(scores * dist)
                sums[2 * h + 1] = sums[2 * h + 1] + fold(scores * order)
                sides.append(scores.astype(LOW))
            scores_low = jnp.concatenate(sides, axis=1)
            grad_values[window, :] += nn(probs_low, grads)
            grad_keys[window, :] += nn(scores_low, queries)
            grad_queries = (pair_pick(tn(scores_low, keys[window, :])) * 0.125).astype(LOW)
            dq_ref[0, lanes, :] = grad_queries
            all_q[row, lanes, cols] = grad_queries
        dk = grad_keys[pl.ds(RADIUS, tokens), :].astype(LOW)
        dv = grad_values[pl.ds(RADIUS, tokens), :].astype(LOW)
        dk_ref[0], all_k[row, :, cols] = dk, dk
        dv_ref[0], all_v[row, :, cols] = dv, dv
        for k in range(4):
            rate_ref[0, 0, k] = sums[k]

    for k, ref in enumerate((all_q, all_k, all_v)):
        @pl.when(step == turns + k)
        def _(ref=ref):
            flat = lambda v: v.reshape(-1, v.shape[-1])
            grad_qkv_ref[...] = tn(flat(low_ref[...]), flat(ref[...])).astype(LOW)

    if remote:
        def last():
            copies = []
            for k, (group, part) in enumerate(zip((out, up), parts)):
                group.fold(1, go=False)
                for side, (y, x) in enumerate(((place.first_y, place.first_x), (place.y, place.x))):
                    copies.append(pltpu.make_async_copy(group.total.at[:, y, x], part.at[side], part_sem.at[2 * k + side]))
                    copies[-1].start()
            down_ref[...] = down.finish()
            down.sent()
            out.sent(2)
            up.sent(2)
            for copy in copies:
                copy.wait()

        when(turns + 2, last)


def attention_backward(remote, depth, qkv, grad, probs, far, order, low, sources):
    pairs, rows, tokens = qkv.shape[0] // 3, qkv.shape[1], qkv.shape[2]
    width = pairs * BLOCK
    blocks = tokens // BLOCK
    turns = rows * pairs
    where = lambda s: (jnp.minimum(s, turns - 1) // pairs, jnp.minimum(s, turns - 1) % pairs)
    row_of, pair_of = lambda s: where(s)[0], lambda s: where(s)[1]
    part = lambda k: pl.BlockSpec((1, 1, tokens, BLOCK), lambda s: (k * pairs + pair_of(s), row_of(s), 0, 0))
    flat = pl.BlockSpec((1, tokens, BLOCK), lambda s: (row_of(s), 0, pair_of(s)))
    bias = pl.BlockSpec((1, blocks, SPAN, BLOCK), lambda s: (row_of(s), 0, 0, 0))
    grads = jax.ShapeDtypeStruct((rows, tokens, width), LOW)
    in_specs = [part(0), part(1), part(2), flat]
    in_specs += [pl.BlockSpec((1, 1, blocks, SPAN, 2 * BLOCK), lambda s: where(s) + (0, 0, 0)), bias, bias, whole(low.shape)]
    out_specs = [flat] * 3 + [
        pl.BlockSpec((1, 1, 4, 8, BLOCK), lambda s: where(s) + (0, 0, 0)),
        pl.BlockSpec((width, width), lambda s: (0, jnp.clip(s - turns, 0, 2))),
    ]
    out_shape = [grads] * 3 + [
        jax.ShapeDtypeStruct((rows, pairs, 4, 8, BLOCK), F32),
        jax.ShapeDtypeStruct((width, 3 * width), LOW),
    ]
    scratch = [pltpu.VMEM((tokens + 2 * RADIUS, BLOCK), LOW)] * 2
    scratch += [pltpu.VMEM((tokens + 2 * RADIUS, BLOCK), F32)] * 2
    scratch += [pltpu.VMEM((rows, tokens, width), LOW)] * 3
    more = {}
    if remote:
        in_specs += [pl.BlockSpec(memory_space=pl.ANY)] * 3
        for k, source in enumerate(sources):
            shape = source.shape[4:]
            if k == 0:
                out_specs.append(pl.BlockSpec(shape, lambda s: (0, 0)))
                out_shape.append(jax.ShapeDtypeStruct(shape, F32))
            else:
                out_specs.append(pl.BlockSpec(memory_space=pl.ANY))
                out_shape.append(jax.ShapeDtypeStruct((2, depth) + shape, LOW))
            scratch += scatter_room(depth, *shape)
        scratch += [pltpu.SemaphoreType.DMA((3, depth + 3))] * 2 + [pltpu.SemaphoreType.DMA((3,)), pltpu.SemaphoreType.DMA((4,))]
        more = {"collective_id": CALLS["attention"], "has_side_effects": True}
    return pl.pallas_call(
        functools.partial(attention_back_kernel, remote, pairs),
        grid=(turns + 3,),
        in_specs=in_specs,
        out_specs=out_specs,
        out_shape=out_shape,
        scratch_shapes=scratch,
        compiler_params=params(1, **more),
        name="attention_backward",
    )(qkv, qkv, qkv, grad, probs, far, order, low, *(sources if remote else ()))


def graph_back_kernel(remote, *refs):
    (dq_in, dk_in, dv_in, two_in, unit_in, rstd_in, slope_in, hidden_in, agg2_in, agg1_in, x_in, adj_in, cols_in,
     first_in, second_in, qkv_w_in, gain_ref, late_ref, rate_ref) = refs[:19]
    refs = refs[19:]
    (qkv_source, *parts), refs = (refs[:3], refs[3:]) if remote else ((None,), refs)
    (input_grad_out, edge_out, gains_out, shifts_out, rates_out), refs = refs[:5], refs[5:]
    owned, refs = (refs[:7], refs[7:]) if remote else (refs[:2], refs[2:])
    (dq, dk, dv, two, unit, rstd, slope, hidden, agg2, adj, cols, first_w, second_w, qkv_w,
     back, norms, edge_sums, row_sem, in_sem, out_sem), refs = refs[:20], refs[20:]
    rows, tokens, width = dq.shape
    blocks, chunk = tokens // BLOCK, 2 * BLOCK
    chunks = tokens // chunk
    agg1, x, branch, mean, pre, one = agg2, hidden, dq, dk, dv, two

    by_row = [(dq_in, dq), (dk_in, dk), (dv_in, dv), (two_in, two), (unit_in, unit), (rstd_in, rstd)]
    row_load = lambda k, row: pltpu.make_async_copy(by_row[k][0].at[row], by_row[k][1].at[row], row_sem.at[k, row])
    once = [(qkv_w_in, qkv_w), (second_in, second_w), (cols_in, cols), (hidden_in, hidden), (agg2_in, agg2),
            (adj_in, adj), (slope_in, slope), (first_in, first_w), (x_in, x), (agg1_in, agg1)]
    load = lambda k: pltpu.make_async_copy(*once[k], in_sem.at[k])
    load(0).start()
    for k in range(len(by_row)):
        row_load(k, 0).start()
    load(1).start()
    load(2).start()
    for row in range(1, rows):
        for k in range(len(by_row)):
            row_load(k, row).start()
    for k in range(3, 8):
        load(k).start()

    if remote:
        rooms = [refs[5 * g : 5 * g + 5] for g in range(3)]
        sums, s_land, s_far, send, recv, own_sem, s_send, s_recv = refs[15:23]
        tails = (refs[23:26], refs[26:29])
        depth = rooms[0][0].shape[0]
        place = Place(depth)
        own = pltpu.make_async_copy(qkv_source.at[:, :, place.core], rooms[0][0], own_sem.at[0])
        qkv = Scatter(place, qkv_source.at[:, :, 1 - place.core], rooms[0], send, recv, 0)
        late, early = [
            Scatter(place, room[0].at[1], (room[0].at[0],) + tuple(room[1:]), send, recv, 1 + g)
            for g, room in enumerate(rooms[1:])
        ]
        out, up = [
            Tail(place, part, room, send, recv, own_sem, 3 + g)
            for g, (part, room) in enumerate(zip(parts, tails))
        ]
        own.start()
        out.load.start()
        up.load.start()
        meet(place)
        qkv.start(0)
        out.across.start()
        up.across.start()

    norms[...] = jnp.zeros_like(norms)
    edge_sums[...] = jnp.zeros_like(edge_sums)
    flat = lambda ref: ref[...].reshape(rows * tokens, width)

    def weight_grad(dest, col, left, right):
        half = width // 2
        for part in range(2):
            grad = tn(left[:, :, part * half : (part + 1) * half].reshape(rows * tokens, half), flat(right))
            if not remote:
                dest[part * half : (part + 1) * half, col * width : (col + 1) * width] = grad.astype(LOW)
                continue
            share = dest.shape[4]
            for k in range(half // share):
                index = part * (half // share) + k
                z, y, core, x_at = index // 8, index // 4 % 2, index // 2 % 2, index % 2
                side = place.core if core == 0 else 1 - place.core
                dest[side, z, y, x_at, :, col * width : (col + 1) * width] = grad[k * share : (k + 1) * share].astype(LOW)

    def spread(row, source):
        back[...] = jnp.zeros_like(back)
        for b in range(blocks):
            back[b * BLOCK : b * BLOCK + WIDE, :] += nn(adj[row, b], source[row, b * BLOCK : (b + 1) * BLOCK, :])

    load(0).wait()
    load(1).wait()
    load(2).wait()

    @pl.loop(0, rows)
    def _(row):
        for k in range(len(by_row)):
            row_load(k, row).wait()
        for c in range(chunks):
            part = slice(c * chunk, (c + 1) * chunk)
            grad = two[row, part, :]
            for k, ref in enumerate((dq, dk, dv)):
                grad = grad + nt(ref[row, part, :], qkv_w[:, k * width : (k + 1) * width])
            plain = unit[row, part, :].astype(F32)
            norms[0] += fold(grad * plain)
            norms[1] += fold(grad)
            grad = norm_back(grad, plain, rstd[row, part, :], gain_ref[0:1, :])
            one[row, part, :] = grad
            low = grad.astype(LOW)
            branch[row, part, :] = low
            mean[row, part, :] = (nt(low, second_w[:, width : 2 * width]) * cols[row, part, 2:3]).astype(LOW)
            if remote and c == 0:
                @pl.when(row == 0)
                def _():
                    own.wait()
                    qkv.fold(0)

    load(3).wait()
    load(4).wait()
    second_dest, first_dest = (rooms[1][0], rooms[2][0]) if remote else (owned[1], owned[0])
    weight_grad(second_dest, 0, hidden, branch)
    weight_grad(second_dest, 1, agg2, branch)
    load(8).start()
    load(9).start()
    if remote:
        late.start(0)
        out.fold()
        up.fold()
        qkv.fold(1)
    for k in range(5, 8):
        load(k).wait()

    @pl.loop(0, rows)
    def _(row):
        spread(row, mean)
        for c in range(chunks):
            part = slice(c * chunk, (c + 1) * chunk)
            grad = back[REACH + c * chunk : REACH + (c + 1) * chunk, :]
            grad = grad + nt(branch[row, part, :], second_w[:, 0:width])
            grad = grad * slope[row, part, :].astype(F32)
            edge_sums[0] += fold(grad * cols[row, part, 0:1])
            edge_sums[1] += fold(grad * cols[row, part, 1:2])
            low = grad.astype(LOW)
            pre[row, part, :] = low
            mean[row, part, :] = (nt(low, first_w[:, width : 2 * width]) * cols[row, part, 2:3]).astype(LOW)
            if remote and c == 0:
                @pl.when(row == 0)
                def _():
                    late.fold(0)
    load(8).wait()
    load(9).wait()
    weight_grad(first_dest, 0, x, pre)
    weight_grad(first_dest, 1, agg1, pre)

    line = lambda v: jnp.sum(v, axis=0, keepdims=True)
    lines = jnp.concatenate(
        [line(edge_sums[0]), line(edge_sums[1]), line(norms[0]), line(late_ref[0]), line(late_ref[2]),
         line(norms[1]), line(late_ref[1]), line(late_ref[3])], axis=0,
    )
    rates = jnp.sum(jnp.sum(rate_ref[...], axis=0), axis=2).reshape(-1, BLOCK)

    if remote:
        early.start(0)
        pieces = width // BLOCK
        for k in range(pieces):
            sums[0, k] = lines[:, k * BLOCK : (k + 1) * BLOCK]
        for k in range(3):
            sums[0, pieces + k] = rates[8 * k : 8 * (k + 1)]
        turns = [
            (sums.at[k], s_land.at[k], k, device)
            for k, device in enumerate((
                place.at(place.z, place.y, 1 - place.core, place.x),
                place.at(place.z, place.y, place.core, 1 - place.x),
                place.at(place.z, 1 - place.y, place.core, place.x),
            ))
        ] + [
            (s_far.at[place.z], s_far.at[place.z], 2 + k, place.at(place.along(k), place.y, place.core, place.x))
            for k in range(1, depth)
        ]
        turns = [
            pltpu.make_async_remote_copy(
                src_ref=source, dst_ref=land, send_sem=s_send.at[slot], recv_sem=s_recv.at[slot],
                device_id=device, device_id_type=pl.DeviceIdType.MESH,
            )
            for source, land, slot, device in turns
        ]
        turns[0].start()
        qkv.fold(2)
        late.fold(1)

    writes = lambda row: pltpu.make_async_copy(one.at[row], input_grad_out.at[row], out_sem.at[row])

    @pl.loop(0, rows)
    def _(row):
        spread(row, mean)
        for c in range(chunks):
            part = slice(c * chunk, (c + 1) * chunk)
            grad = one[row, part, :] + back[REACH + c * chunk : REACH + (c + 1) * chunk, :]
            one[row, part, :] = grad + nt(pre[row, part, :], first_w[:, 0:width])
            if remote and c == 0:
                @pl.when(row == 0)
                def _():
                    early.fold(0)
                    turns[0].wait_recv()
                    sums[1] = sums[0] + s_land[0]
                    turns[1].start()
        writes(row).start()

    if remote:
        turns[1].wait_recv()
        sums[2] = sums[1] + s_land[1]
        turns[2].start()
        late.fold(2)
        early.fold(1)
        turns[2].wait_recv()
        s_far[place.z] = sums[2] + s_land[2]
        for turn in turns[3:]:
            turn.start()
        owned[5][...] = out.finish()
        owned[6][...] = up.finish()
        owned[4][...] = qkv.finish()
        early.fold(2)
        result = late.finish()
        owned[2][...] = result[:, :width]
        owned[3][...] = result[:, width:]
        for turn in turns[3:]:
            turn.wait_recv()
        total = s_far[0]
        for k in range(1, depth):
            total = total + s_far[k]
        for k in range(pieces):
            part = slice(k * BLOCK, (k + 1) * BLOCK)
            edge_out[:, part] = total[k, 0:2]
            gains_out[:, part] = total[k, 2:5]
            shifts_out[:, part] = total[k, 5:8]
        for k in range(3):
            rates_out[8 * k : 8 * (k + 1)] = jnp.sum(total[pieces + k], axis=1, keepdims=True)
        result = early.finish()
        owned[0][...] = result[:, :width]
        owned[1][...] = result[:, width:]
        for group in (qkv, late, early):
            group.sent()
        for turn in turns:
            turn.wait_send()
    else:
        edge_out[...], gains_out[...], shifts_out[...] = lines[0:2], lines[2:5], lines[5:8]
        rates_out[...] = jnp.sum(rates, axis=1, keepdims=True)
    for row in range(rows):
        writes(row).wait()


def graph_backward(remote, depth, arrays, gains, late, rates, sources):
    dq, two, unit, rstd, slope, hidden, adj, cols = (arrays[k] for k in (0, 3, 4, 5, 6, 7, 11, 12))
    rows, tokens, width = dq.shape
    vmem, hbm = pl.BlockSpec(memory_space=pltpu.VMEM), pl.BlockSpec(memory_space=pl.ANY)
    shape = lambda dtype, *dims: jax.ShapeDtypeStruct(dims, dtype)
    out_shape = [
        shape(F32, rows, tokens, width), shape(F32, 2, width), shape(F32, 3, width), shape(F32, 3, width),
        shape(F32, rates.shape[1] * 4, 1),
    ]
    like = lambda v: pltpu.VMEM(v.shape, v.dtype)
    scratch = [like(v) for v in (dq, dq, dq, two, unit, rstd, slope, hidden, hidden, adj, cols) + tuple(arrays[13:16])]
    scratch += [
        pltpu.VMEM((tokens + 2 * REACH, width), F32),
        pltpu.VMEM((2, 8, width), F32),
        pltpu.VMEM((2, 8, width), F32),
        pltpu.SemaphoreType.DMA((6, rows)),
        pltpu.SemaphoreType.DMA((10,)),
        pltpu.SemaphoreType.DMA((rows,)),
    ]
    more = {}
    if remote:
        share = sources[0].shape[4]
        out_shape += [shape(F32, share, width)] * 4 + [shape(F32, share, s.shape[-1]) for s in sources]
        scratch += scatter_room(depth, share, sources[0].shape[5])
        for _ in range(2):
            scratch += scatter_room(depth, share, 2 * width, (2,))
        lines = (width // BLOCK + 3, 8, BLOCK)
        scratch += [pltpu.VMEM((3,) + lines, F32), pltpu.VMEM((3,) + lines, F32), pltpu.VMEM((depth,) + lines, F32)]
        scratch += [pltpu.SemaphoreType.DMA((5, depth + 3))] * 2 + [pltpu.SemaphoreType.DMA((5,))]
        scratch += [pltpu.SemaphoreType.DMA((depth + 2,))] * 2
        for part in sources[1:]:
            scratch += [pltpu.VMEM((k, share, part.shape[3]), LOW) for k in (depth, depth, depth - 1)]
        more = {"collective_id": CALLS["graph"], "has_side_effects": True}
    else:
        out_shape += [shape(LOW, width, 2 * width)] * 2
    return pl.pallas_call(
        functools.partial(graph_back_kernel, remote),
        in_specs=[hbm] * 16 + [vmem] * 3 + [hbm] * (3 if remote else 0),
        out_specs=[hbm] + [vmem] * (len(out_shape) - 1),
        out_shape=out_shape,
        scratch_shapes=scratch,
        compiler_params=pltpu.CompilerParams(vmem_limit_bytes=VMEM, **more),
        name="graph_backward",
    )(*arrays, gains, late, rates, *(sources if remote else ()))


def local(
    sizes, inputs, coords, neighbours, counts, doc_length, self_one, near_one, self_two, near_two, edge_proj,
    qkv_proj, out_proj, up_proj, down_proj, norm_gains, norm_shifts, distance_rate, order_rate, cotangent,
):
    axes = ("wide", "narrow")
    rows, tokens, width = inputs.shape
    wide_size, narrow_size = sizes
    depth = wide_size // 4
    remote = wide_size % 4 == 0 and narrow_size == 2 and self_one.shape[0] % 8 == 0
    weights, shards = (self_one, near_one, self_two, near_two, qkv_proj), (out_proj, up_proj, down_proj)
    gather = lambda v: lax.all_gather(v, axes, axis=0, tiled=True)
    scatter = lambda v: lax.psum_scatter(v, axes, scatter_dimension=0, tiled=True).astype(F32)
    blocked = lambda v: v.reshape(depth, 2, 2, 2, -1, v.shape[1])
    flat = lambda v: v.reshape(rows * tokens, width)
    tall = lambda v: v.reshape(rows, tokens, width)
    if not remote:
        weights, shards = tuple(map(gather, weights)), tuple(map(gather, shards))
    results = front(
        remote, depth, doc_length[:, 0], distance_rate, order_rate, neighbours, counts[:, None, :], coords, inputs,
        edge_proj, norm_gains, norm_shifts, weights, shards if remote else (),
    )
    (adj, cols, agg1, slope, hidden, agg2, unit, rstd, normed, low, qkv, att, probs, far, order, first_w, second_w, qkv_w) = results[:18]
    out_w, up = (v.reshape(-1, v.shape[-1]) for v in results[18:20]) if remote else shards[:2]
    result, two, grad_att, grad_out, grad_up, grad_down, late = block_both(
        remote, depth, att.reshape(-1, rows * tokens, BLOCK), flat(normed), flat(cotangent), out_w, up, results[20] if remote else shards[2],
        norm_gains, norm_shifts,
    )
    first_sources = (blocked(grad_down), blocked(grad_out), blocked(grad_up)) if remote else ()
    dq, dk, dv, rates, grad_qkv, *summed = attention_backward(
        remote, depth, qkv, tall(grad_att), probs, far, order, low, first_sources
    )
    arrays = (dq, dk, dv, tall(two), unit, rstd, slope, hidden, agg2, agg1, inputs, adj, cols, first_w, second_w, qkv_w)
    sources = (blocked(grad_qkv), summed[1], summed[2]) if remote else ()
    input_grad, edge, gains, shifts, rates, *owned = graph_backward(remote, depth, arrays, norm_gains, late, rates, sources)
    if remote:
        down_own = summed[0]
        self1, near1, self2, near2, qkv_own, out_own, up_own = owned
    else:
        down_own, out_own, up_own, qkv_own = map(scatter, (grad_down, grad_out, grad_up, grad_qkv))
        self1, near1 = jnp.split(scatter(owned[0]), 2, axis=1)
        self2, near2 = jnp.split(scatter(owned[1]), 2, axis=1)
        edge, gains, shifts, rates = lax.psum((edge, gains, shifts, rates), axes)
    rates = rates.reshape(-1, 2, 2)
    return (
        tall(result), input_grad, self1, near1, self2, near2, edge, qkv_own, out_own, up_own, down_own, gains, shifts,
        rates[:, :, 0].reshape(-1), rates[:, :, 1].reshape(-1),
    )


def solution(mesh):
    axes = ("wide", "narrow")
    middle, last = P(None, axes, None), P(None, None, axes)
    count, weight, same = P(None, axes), P(axes, None), P()
    sizes = (mesh.shape["wide"], mesh.shape["narrow"])
    return jax.shard_map(
        functools.partial(local, sizes),
        mesh=mesh,
        in_specs=(middle, last, last, count, count)
        + (weight,) * 4
        + (same,)
        + (weight,) * 4
        + (same,) * 4
        + (middle,),
        out_specs=(middle, middle) + (weight,) * 4 + (same,) + (weight,) * 4 + (same,) * 4,
        check_vma=False,
    )
```

profile of v0, /device:TPU:0, one launch (start us, length us, event | category | flops | bytes accessed | tf_op | source)
XLA Modules:
  0.0 344.4 jit_solution(18164304400686275164)
XLA Ops:
  0.6 1.3 broadcast_in_dim.3.refs_4_
  1.9 95.5 %front.1 = (bf16[2,6,256,128]{3,2,1,0:T(8,128)(2,1)}, f32[2,768,8]{2,1,0:T(8,128)}, bf16[2,768,768]{2,1,0:T(8,128)(2,1)}, bf16[2,768,768]{2,1,0:T(8,128)(2,1)}, ...) custom-call(s32[2]{0:T(128)} %bitcast.25, ...), custom_call_target="tpu_custom_call" | custom-call | tf_op jit(solution)/shard_map/front/pallas_call | solution.py:534
  97.4 101.3 %block_both.1 = (bf16[1536,768]{1,0:T(8,128)(2,1)}, f32[1536,768]{1,0:T(8,128)}, bf16[1536,768]{1,0:T(8,128)(2,1)}, bf16[768,768]{1,0:T(8,128)(2,1)}, bf16[768,3...) custom-call(bf16[6,1536,128]{2,1,0:T(8,128)(2,1)} %bitcast.21, f32[1536,768]{1,0:T(8,128)} %bitcast.14, ...), custom_call_target="tpu_custom_call" | custom-call | tf_op jit(solution)/shard_map/block_both/pallas_call | solution.py:710
  198.8 60.4 %attention_backward.1 = (bf16[2,768,768]{2,1,0:T(8,128)(2,1)}, bf16[2,768,768]{2,1,0:T(8,128)(2,1)}, bf16[2,768,768]{2,1,0:T(8,128)(2,1)}, f32[2,6,4,8,128]{4,3,...) custom-call(bf16[18,2,768,128]{3,2,1,0:T(8,128)(2,1)} %get-tuple-ele, ...), custom_call_target="tpu_custom_call" | custom-call | tf_op jit(solution)/shard_map/attention_backward/pallas_call | solution.py:1022
  259.1 70.0 %graph_backward.1 = (f32[2,768,768]{2,1,0:T(8,128)}, f32[2,768]{1,0:T(2,128)}, f32[3,768]{1,0:T(4,128)}, f32[3,768]{1,0:T(4,128)}, f32[24,1]{1,0:T(8,128)}, /*in...) custom-call(bf16[2,768,768]{2,1,0:T(8,128)(2,1)} %get-tuple-element., ...), custom_call_target="tpu_custom_call" | custom-call | tf_op jit(solution)/shard_map/graph_backward/pallas_call | solution.py:1307
  329.1 0.8 reduce
  330.0 0.1 reshape.81
  330.0 0.1 slice_reduce_fusion
  330.2 0.6 reshape_squeeze.7
  330.8 0.6 reshape_squeeze.6
  331.4 0.0 copy-start
  331.4 3.4 copy.47
  334.8 0.0 copy-done
  334.8 0.0 copy-start.8
  334.8 0.0 copy-start.7
  334.8 0.0 copy-start.6
  334.8 0.0 copy-start.5
  334.8 0.0 copy-start.11
  334.8 0.0 copy-start.3
  334.8 0.0 copy-start.4
  334.8 0.0 copy-start.2
  334.8 0.0 copy-start.1
  334.9 2.2 copy.48
  337.0 0.0 copy-done.8
  337.0 0.0 copy-start.10
  337.1 0.0 copy-start.9
  337.1 0.6 copy.49
  337.7 0.0 copy-done.7
  337.7 0.6 copy.50
  338.3 0.0 copy-done.6
  338.3 0.6 copy.51
  339.0 0.0 copy-done.5
  339.0 0.6 copy.52
  339.6 0.0 copy-done.11
  339.6 0.6 copy.53
  340.2 0.0 copy-done.3
  340.2 0.7 copy.54
  340.9 0.0 copy-done.4
  340.9 0.6 copy.55
  341.5 0.0 copy-done.2
  341.5 0.7 copy.56
  342.2 0.0 copy-done.1
  342.2 0.7 copy.57
  342.9 0.0 copy-done.10
  343.0 0.6 copy.58
  343.6 0.0 copy-done.9
  343.6 0.6 copy.59
Async XLA Ops:
  331.4 3.4 copy-start
  334.8 2.3 copy-start.8
  334.8 2.9 copy-start.7
  334.8 3.5 %copy-start.6 = (f32[24,768]{1,0:T(8,128)S(1)}, f32[24,768]{1,0:T(8,128)}, u32[]{:S(2)}) copy-start(f32[24,768]{1,0:T(8,128)} %get-tuple-element.132) | copy-start | bytes 221188
  334.8 4.2 %copy-start.5 = (f32[24,768]{1,0:T(8,128)S(1)}, f32[24,768]{1,0:T(8,128)}, u32[]{:S(2)}) copy-start(f32[24,768]{1,0:T(8,128)} %get-tuple-element.133) | copy-start | bytes 221188
  334.8 4.8 %copy-start.11 = (f32[2,768]{1,0:T(2,128)S(1)}, f32[2,768]{1,0:T(2,128)}, u32[]{:S(2)}) copy-start(f32[2,768]{1,0:T(2,128)} %get-tuple-element.134) | copy-start | bytes 18436
  334.8 5.4 %copy-start.3 = (f32[24,2304]{1,0:T(8,128)S(1)}, f32[24,2304]{1,0:T(8,128)}, u32[]{:S(2)}) copy-start(f32[24,2304]{1,0:T(8,128)} %get-tuple-element.135) | copy-start | bytes 663556
  334.8 6.1 %copy-start.4 = (f32[24,768]{1,0:T(8,128)S(1)}, f32[24,768]{1,0:T(8,128)}, u32[]{:S(2)}) copy-start(f32[24,768]{1,0:T(8,128)} %get-tuple-element.136) | copy-start | bytes 221188
  334.8 6.7 %copy-start.2 = (f32[24,3072]{1,0:T(8,128)S(1)}, f32[24,3072]{1,0:T(8,128)}, u32[]{:S(2)}) copy-start(f32[24,3072]{1,0:T(8,128)} %get-tuple-element.137) | copy-start | bytes 884740
  334.8 7.4 %copy-start.1 = (f32[96,768]{1,0:T(8,128)S(1)}, f32[96,768]{1,0:T(8,128)}, u32[]{:S(2)}) copy-start(f32[96,768]{1,0:T(8,128)} %get-tuple-element.138) | copy-start | bytes 884740
  337.0 5.9 %copy-start.10 = (f32[3,768]{1,0:T(4,128)S(1)}, f32[3,768]{1,0:T(4,128)}, u32[]{:S(2)}) copy-start(f32[3,768]{1,0:T(4,128)} %get-tuple-element.139) | copy-start | bytes 27652
  337.1 6.5 %copy-start.9 = (f32[3,768]{1,0:T(4,128)S(1)}, f32[3,768]{1,0:T(4,128)}, u32[]{:S(2)}) copy-start(f32[3,768]{1,0:T(4,128)} %get-tuple-element.140) | copy-start | bytes 27652
where the time goes:
time: 347 us; the launch traced here: 344 us
  Pallas kernels  327 us (94%)
  local copies, waits for them, and re-layouts  15.4 us (4%)
    pallas_call x1, Pallas kernels, block_both(): pl.pallas_call(functools.partial(block_kernel, remote, steps), grid=(2 *...  101 us
    pallas_call x1, Pallas kernels, front(): pl.pallas_call(functools.partial(front_kernel, remote), in_specs=[smem] *...  95.5 us
    pallas_call x1, Pallas kernels, graph_backward(): pl.pallas_call(functools.partial(graph_back_kernel, remote), in_specs=[hb...  70 us
    pallas_call x1, Pallas kernels, attention_backward(): pl.pallas_call(functools.partial(attention_back_kernel, remote, pairs), g...  60.4 us
    unnamed x37, local copies, waits for them, and re-layouts  12.7 us

commit v1 on v0

--- a/solution.py
+++ b/solution.py
@@ -546,19 +546,22 @@
 
 
 def block_kernel(remote, steps, *refs):
-    (att_ref, normed_in, cot_ref, out_w_ref, up_ref, down_in, gain_ref, shift_ref,
+    (att_ref, normed_in, cot_ref, out_w_ref, up_in, down_in, gain_ref, shift_ref,
      result_ref, two_out, grad_att_ref, grad_out_out, grad_up_ref, grad_down_ref, norms_ref,
-     act_all, up_all, second_all, down_all, attn_all, normed_all, unit_all, rstd_all, down_w, in_sem, out_sem) = refs[:26]
+     act_all, up_all, second_all, down_all, attn_all, normed_all, unit_all, rstd_all, down_w, up_ref, in_sem, normed_sem, up_sem, out_sem) = refs[:29]
     step = pl.program_id(0)
     turns, tokens, half = act_all.shape
     parts, piece = turns // 2, 2 * half
     width = normed_all.shape[1]
-    load = pltpu.make_async_copy(normed_in, normed_all, in_sem.at[0])
+    tile = lambda k: pl.ds(pl.multiple_of(k * TILE, TILE), TILE)
+    load_normed = lambda k: pltpu.make_async_copy(normed_in.at[tile(k)], normed_all.at[tile(k)], normed_sem.at[k])
+    chunk = lambda c: (slice(None), pl.ds(c * piece, piece))
+    load_up = [pltpu.make_async_copy(up_in.at[chunk(c)], up_ref.at[chunk(c)], up_sem.at[c]) for c in range(parts)]
     write_two = pltpu.make_async_copy(normed_all, two_out, out_sem.at[0])
     write_out = pltpu.make_async_copy(unit_all.at[pl.ds(0, width)], grad_out_out, out_sem.at[1])
 
     if remote:
-        send, recv = refs[26:]
+        send, recv = refs[29:]
         place = Place(parts)
         mine, first, second, last = [
             down_w.at[:, y, place.core, x]
@@ -625,14 +628,18 @@
 
     @pl.when(step == 0)
     def _():
-        load.start()
+        load_normed(0).start()
+        for copy_up in load_up:
+            copy_up.start()
+        for k in range(1, steps):
+            load_normed(k).start()
         norms_ref[...] = jnp.zeros_like(norms_ref)
         begin()
-        load.wait()
 
     @pl.when(step < steps)
     def _():
-        at = pl.ds(pl.multiple_of(step * TILE, TILE), TILE)
+        at = tile(step)
+        load_normed(step).wait()
         att = jnp.concatenate([att_ref[k, at, :] for k in range(att_ref.shape[0])], axis=1)
         unit, rstd = norm_parts(normed_all[at, :] + nn(att, out_w_ref[...]))
         unit_all[at, :] = unit.astype(LOW)
@@ -641,6 +648,7 @@
         normed_all[at, :] = normed
         second_all[at, :] = normed.astype(LOW)
         for c in range(parts):
+            pl.when(step == 0)(load_up[c].wait)
             act, deriv = gelu_pair(nn(second_all[at, :], up_ref[:, c * piece : (c + 1) * piece]))
             put(act_all, c, at, act.astype(LOW))
             put(up_all, c, at, deriv.astype(LOW))
@@ -711,7 +719,7 @@
         functools.partial(block_kernel, remote, steps),
         grid=(2 * steps + 2 * parts,),
         in_specs=[
-            whole(att.shape), hbm, tile, whole((width, width)), whole(up.shape), hbm, whole(gains.shape), whole(shifts.shape),
+            whole(att.shape), hbm, tile, whole((width, width)), hbm, hbm, whole(gains.shape), whole(shifts.shape),
         ],
         out_specs=[
             tile, hbm, tile, hbm,
@@ -734,7 +742,10 @@
             tall_low,
             pltpu.VMEM((tokens, 1), F32),
             pltpu.VMEM(down.shape, LOW),
+            pltpu.VMEM(up.shape, LOW),
             pltpu.SemaphoreType.DMA((4,)),
+            pltpu.SemaphoreType.DMA((steps,)),
+            pltpu.SemaphoreType.DMA((parts,)),
             pltpu.SemaphoreType.DMA((2,)),
         ]
         + ([pltpu.SemaphoreType.DMA((5,))] * 2 if remote else []),
@@ -907,15 +918,11 @@
             groups[k].fold(0, go)
 
         when(0, begin)
-        def second():
-            down.fold(1)
-            out.start(1)
-            up.start(1)
-
         when(1, lambda: (first(0), out.start(0), up.start(0)))
         when(3, lambda: (first(1, False), first(2, False)))
-        when(7, second)
-        when(11, lambda: down.fold(2))
+        when(6, lambda: down.fold(1))
+        when(8, lambda: (out.start(1), up.start(1)))
+        when(10, lambda: down.fold(2))
 
     @pl.when(step < turns)
     def _():
@@ -1062,19 +1069,19 @@
         load(k).start()
 
     if remote:
-        rooms = [refs[5 * g : 5 * g + 5] for g in range(3)]
-        sums, s_land, s_far, send, recv, own_sem, s_send, s_recv = refs[15:23]
-        tails = (refs[23:26], refs[26:29])
+        rooms = [refs[5 * g : 5 * g + 5] for g in range(4)]
+        sums, s_land, s_far, send, recv, own_sem, s_send, s_recv = refs[20:28]
+        tails = (refs[28:31], refs[31:34])
         depth = rooms[0][0].shape[0]
         place = Place(depth)
         own = pltpu.make_async_copy(qkv_source.at[:, :, place.core], rooms[0][0], own_sem.at[0])
         qkv = Scatter(place, qkv_source.at[:, :, 1 - place.core], rooms[0], send, recv, 0)
-        late, early = [
+        late, early, final = [
             Scatter(place, room[0].at[1], (room[0].at[0],) + tuple(room[1:]), send, recv, 1 + g)
             for g, room in enumerate(rooms[1:])
         ]
         out, up = [
-            Tail(place, part, room, send, recv, own_sem, 3 + g)
+            Tail(place, part, room, send, recv, own_sem, 4 + g)
             for g, (part, room) in enumerate(zip(parts, tails))
         ]
         own.start()
@@ -1162,7 +1169,6 @@
             edge_sums[1] += fold(grad * cols[row, part, 1:2])
             low = grad.astype(LOW)
             pre[row, part, :] = low
-            mean[row, part, :] = (nt(low, first_w[:, width : 2 * width]) * cols[row, part, 2:3]).astype(LOW)
             if remote and c == 0:
                 @pl.when(row == 0)
                 def _():
@@ -1170,7 +1176,9 @@
     load(8).wait()
     load(9).wait()
     weight_grad(first_dest, 0, x, pre)
-    weight_grad(first_dest, 1, agg1, pre)
+    if remote:
+        early.start(0)
+    weight_grad(rooms[3][0] if remote else first_dest, 0 if remote else 1, agg1, pre)
 
     line = lambda v: jnp.sum(v, axis=0, keepdims=True)
     lines = jnp.concatenate(
@@ -1180,7 +1188,8 @@
     rates = jnp.sum(jnp.sum(rate_ref[...], axis=0), axis=2).reshape(-1, BLOCK)
 
     if remote:
-        early.start(0)
+        final.start(0)
+        early.fold(0)
         pieces = width // BLOCK
         for k in range(pieces):
             sums[0, k] = lines[:, k * BLOCK : (k + 1) * BLOCK]
@@ -1212,26 +1221,34 @@
 
     @pl.loop(0, rows)
     def _(row):
+        for c in range(chunks):
+            part = slice(c * chunk, (c + 1) * chunk)
+            mean[row, part, :] = (nt(pre[row, part, :], first_w[:, width : 2 * width]) * cols[row, part, 2:3]).astype(LOW)
+        if remote:
+            @pl.when(row == 0)
+            def _():
+                final.fold(0)
+                turns[0].wait_recv()
+                sums[1] = sums[0] + s_land[0]
+                turns[1].start()
         spread(row, mean)
         for c in range(chunks):
             part = slice(c * chunk, (c + 1) * chunk)
             grad = one[row, part, :] + back[REACH + c * chunk : REACH + (c + 1) * chunk, :]
             one[row, part, :] = grad + nt(pre[row, part, :], first_w[:, 0:width])
-            if remote and c == 0:
-                @pl.when(row == 0)
-                def _():
-                    early.fold(0)
-                    turns[0].wait_recv()
-                    sums[1] = sums[0] + s_land[0]
-                    turns[1].start()
         writes(row).start()
+        if remote:
+            @pl.when(row == 0)
+            def _():
+                early.fold(1)
 
     if remote:
         turns[1].wait_recv()
         sums[2] = sums[1] + s_land[1]
         turns[2].start()
         late.fold(2)
-        early.fold(1)
+        final.fold(1)
+        early.fold(2)
         turns[2].wait_recv()
         s_far[place.z] = sums[2] + s_land[2]
         for turn in turns[3:]:
@@ -1239,7 +1256,7 @@
         owned[5][...] = out.finish()
         owned[6][...] = up.finish()
         owned[4][...] = qkv.finish()
-        early.fold(2)
+        final.fold(2)
         result = late.finish()
         owned[2][...] = result[:, :width]
         owned[3][...] = result[:, width:]
@@ -1255,10 +1272,9 @@
             shifts_out[:, part] = total[k, 5:8]
         for k in range(3):
             rates_out[8 * k : 8 * (k + 1)] = jnp.sum(total[pieces + k], axis=1, keepdims=True)
-        result = early.finish()
-        owned[0][...] = result[:, :width]
-        owned[1][...] = result[:, width:]
-        for group in (qkv, late, early):
+        owned[0][...] = early.finish()
+        owned[1][...] = final.finish()
+        for group in (qkv, late, early, final):
             group.sent()
         for turn in turns:
             turn.wait_send()
@@ -1293,11 +1309,11 @@
         share = sources[0].shape[4]
         out_shape += [shape(F32, share, width)] * 4 + [shape(F32, share, s.shape[-1]) for s in sources]
         scratch += scatter_room(depth, share, sources[0].shape[5])
-        for _ in range(2):
-            scratch += scatter_room(depth, share, 2 * width, (2,))
+        for cols in (2 * width, width, width):
+            scratch += scatter_room(depth, share, cols, (2,))
         lines = (width // BLOCK + 3, 8, BLOCK)
         scratch += [pltpu.VMEM((3,) + lines, F32), pltpu.VMEM((3,) + lines, F32), pltpu.VMEM((depth,) + lines, F32)]
-        scratch += [pltpu.SemaphoreType.DMA((5, depth + 3))] * 2 + [pltpu.SemaphoreType.DMA((5,))]
+        scratch += [pltpu.SemaphoreType.DMA((6, depth + 3))] * 2 + [pltpu.SemaphoreType.DMA((6,))]
         scratch += [pltpu.SemaphoreType.DMA((depth + 2,))] * 2
         for part in sources[1:]:
             scratch += [pltpu.VMEM((k, share, part.shape[3]), LOW) for k in (depth, depth, depth - 1)]

time: 347 us -> 345 us (level)
  no operation moved by 1% of the time
where the time goes in v1:
time: 345 us; the launch traced here: 343 us
  Pallas kernels  325 us (94%)
  local copies, waits for them, and re-layouts  15.4 us (4%)
    pallas_call x1, Pallas kernels, block_both(): pl.pallas_call(functools.partial(block_kernel, remote, steps), grid=(2 *...  102 us
    pallas_call x1, Pallas kernels, front(): pl.pallas_call(functools.partial(front_kernel, remote), in_specs=[smem] *...  95.5 us
    pallas_call x1, Pallas kernels, graph_backward(): pl.pallas_call(functools.partial(graph_back_kernel, remote), in_specs=[hb...  69.4 us
    pallas_call x1, Pallas kernels, attention_backward(): pl.pallas_call(functools.partial(attention_back_kernel, remote, pairs), g...  58.3 us
    unnamed x37, local copies, waits for them, and re-layouts  12.7 us

profile of v1, /device:TPU:0, one launch (start us, length us, event | category | flops | bytes accessed | tf_op | source)
XLA Modules:
  0.0 342.6 jit_solution(17001981015657164890)
XLA Ops:
  0.6 1.3 broadcast_in_dim.3.refs_4_
  1.9 95.5 %front.1 = (bf16[2,6,256,128]{3,2,1,0:T(8,128)(2,1)}, f32[2,768,8]{2,1,0:T(8,128)}, bf16[2,768,768]{2,1,0:T(8,128)(2,1)}, bf16[2,768,768]{2,1,0:T(8,128)(2,1)}, ...) custom-call(s32[2]{0:T(128)} %bitcast.25, ...), custom_call_target="tpu_custom_call" | custom-call | tf_op jit(solution)/shard_map/front/pallas_call | solution.py:534
  97.4 102.2 %block_both.1 = (bf16[1536,768]{1,0:T(8,128)(2,1)}, f32[1536,768]{1,0:T(8,128)}, bf16[1536,768]{1,0:T(8,128)(2,1)}, bf16[768,768]{1,0:T(8,128)(2,1)}, bf16[768,3...) custom-call(bf16[6,1536,128]{2,1,0:T(8,128)(2,1)} %bitcast.21, f32[1536,768]{1,0:T(8,128)} %bitcast.14, ...), custom_call_target="tpu_custom_call" | custom-call | tf_op jit(solution)/shard_map/block_both/pallas_call | solution.py:718
  199.7 58.3 %attention_backward.1 = (bf16[2,768,768]{2,1,0:T(8,128)(2,1)}, bf16[2,768,768]{2,1,0:T(8,128)(2,1)}, bf16[2,768,768]{2,1,0:T(8,128)(2,1)}, f32[2,6,4,8,128]{4,3,...) custom-call(bf16[18,2,768,128]{3,2,1,0:T(8,128)(2,1)} %get-tuple-ele, ...), custom_call_target="tpu_custom_call" | custom-call | tf_op jit(solution)/shard_map/attention_backward/pallas_call | solution.py:1029
  258.0 69.4 %graph_backward.1 = (f32[2,768,768]{2,1,0:T(8,128)}, f32[2,768]{1,0:T(2,128)}, f32[3,768]{1,0:T(4,128)}, f32[3,768]{1,0:T(4,128)}, f32[24,1]{1,0:T(8,128)}, /*in...) custom-call(bf16[2,768,768]{2,1,0:T(8,128)(2,1)} %get-tuple-element., ...), custom_call_target="tpu_custom_call" | custom-call | tf_op jit(solution)/shard_map/graph_backward/pallas_call | solution.py:1323
  327.3 0.8 reduce
  328.2 0.1 reshape.81
  328.3 0.1 slice_reduce_fusion
  328.4 0.6 reshape_squeeze.7
  329.0 0.6 reshape_squeeze.6
  329.6 0.0 copy-start
  329.6 3.4 copy.47
  333.0 0.0 copy-done
  333.0 0.0 copy-start.8
  333.0 0.0 copy-start.7
  333.0 0.0 copy-start.6
  333.0 0.0 copy-start.5
  333.0 0.0 copy-start.11
  333.0 0.0 copy-start.3
  333.0 0.0 copy-start.4
  333.1 0.0 copy-start.2
  333.1 0.0 copy-start.1
  333.1 2.2 copy.48
  335.3 0.0 copy-done.8
  335.3 0.0 copy-start.10
  335.3 0.0 copy-start.9
  335.3 0.6 copy.49
  335.9 0.0 copy-done.7
  335.9 0.6 copy.50
  336.5 0.0 copy-done.6
  336.5 0.6 copy.51
  337.2 0.0 copy-done.5
  337.2 0.6 copy.52
  337.8 0.0 copy-done.11
  337.8 0.6 copy.53
  338.4 0.0 copy-done.3
  338.4 0.7 copy.54
  339.1 0.0 copy-done.4
  339.1 0.6 copy.55
  339.7 0.0 copy-done.2
  339.7 0.7 copy.56
  340.4 0.0 copy-done.1
  340.4 0.7 copy.57
  341.2 0.0 copy-done.10
  341.2 0.6 copy.58
  341.8 0.0 copy-done.9
  341.8 0.6 copy.59
Async XLA Ops:
  329.6 3.4 copy-start
  333.0 2.3 copy-start.8
  333.0 2.9 copy-start.7
  333.0 3.5 %copy-start.6 = (f32[24,768]{1,0:T(8,128)S(1)}, f32[24,768]{1,0:T(8,128)}, u32[]{:S(2)}) copy-start(f32[24,768]{1,0:T(8,128)} %get-tuple-element.132) | copy-start | bytes 221188
  333.0 4.2 %copy-start.5 = (f32[24,768]{1,0:T(8,128)S(1)}, f32[24,768]{1,0:T(8,128)}, u32[]{:S(2)}) copy-start(f32[24,768]{1,0:T(8,128)} %get-tuple-element.133) | copy-start | bytes 221188
  333.0 4.8 %copy-start.11 = (f32[2,768]{1,0:T(2,128)S(1)}, f32[2,768]{1,0:T(2,128)}, u32[]{:S(2)}) copy-start(f32[2,768]{1,0:T(2,128)} %get-tuple-element.134) | copy-start | bytes 18436
  333.0 5.4 %copy-start.3 = (f32[24,2304]{1,0:T(8,128)S(1)}, f32[24,2304]{1,0:T(8,128)}, u32[]{:S(2)}) copy-start(f32[24,2304]{1,0:T(8,128)} %get-tuple-element.135) | copy-start | bytes 663556
  333.0 6.1 %copy-start.4 = (f32[24,768]{1,0:T(8,128)S(1)}, f32[24,768]{1,0:T(8,128)}, u32[]{:S(2)}) copy-start(f32[24,768]{1,0:T(8,128)} %get-tuple-element.136) | copy-start | bytes 221188
  333.1 6.7 %copy-start.2 = (f32[24,3072]{1,0:T(8,128)S(1)}, f32[24,3072]{1,0:T(8,128)}, u32[]{:S(2)}) copy-start(f32[24,3072]{1,0:T(8,128)} %get-tuple-element.137) | copy-start | bytes 884740
  333.1 7.4 %copy-start.1 = (f32[96,768]{1,0:T(8,128)S(1)}, f32[96,768]{1,0:T(8,128)}, u32[]{:S(2)}) copy-start(f32[96,768]{1,0:T(8,128)} %get-tuple-element.138) | copy-start | bytes 884740
  335.3 5.9 %copy-start.10 = (f32[3,768]{1,0:T(4,128)S(1)}, f32[3,768]{1,0:T(4,128)}, u32[]{:S(2)}) copy-start(f32[3,768]{1,0:T(4,128)} %get-tuple-element.139) | copy-start | bytes 27652
  335.3 6.5 %copy-start.9 = (f32[3,768]{1,0:T(4,128)S(1)}, f32[3,768]{1,0:T(4,128)}, u32[]{:S(2)}) copy-start(f32[3,768]{1,0:T(4,128)} %get-tuple-element.140) | copy-start | bytes 27652

commit v2 on v1

--- a/solution.py
+++ b/solution.py
@@ -435,7 +435,7 @@
                 gd.arrive("along")
                 gd.start(FIRST, OWN)
 
-            @pl.when(turn == 6)
+            @pl.when(turn == 8)
             def _():
                 for g in (go, gu):
                     g.arrive(OWN, PASSED)

time: 345 us -> 341 us (0.988)
    pallas_call x1, Pallas kernels: 95.5 us -> 91.7 us  [front(): pl.pallas_call(functools.partial(front_kernel, remote), in_specs=[smem] *...]
where the time goes in v2:
time: 341 us; the launch traced here: 339 us
  Pallas kernels  322 us (94%)
  local copies, waits for them, and re-layouts  15.4 us (5%)
    pallas_call x1, Pallas kernels, block_both(): pl.pallas_call(functools.partial(block_kernel, remote, steps), grid=(2 *...  105 us
    pallas_call x1, Pallas kernels, front(): pl.pallas_call(functools.partial(front_kernel, remote), in_specs=[smem] *...  91.7 us
    pallas_call x1, Pallas kernels, graph_backward(): pl.pallas_call(functools.partial(graph_back_kernel, remote), in_specs=[hb...  69.2 us
    pallas_call x1, Pallas kernels, attention_backward(): pl.pallas_call(functools.partial(attention_back_kernel, remote, pairs), g...  56.6 us
    unnamed x37, local copies, waits for them, and re-layouts  12.7 us

profile of v2, /device:TPU:0, one launch (start us, length us, event | category | flops | bytes accessed | tf_op | source)
XLA Modules:
  0.0 339.2 jit_solution(11697214774077602623)
XLA Ops:
  0.6 1.3 broadcast_in_dim.3.refs_4_
  1.9 91.7 %front.1 = (bf16[2,6,256,128]{3,2,1,0:T(8,128)(2,1)}, f32[2,768,8]{2,1,0:T(8,128)}, bf16[2,768,768]{2,1,0:T(8,128)(2,1)}, bf16[2,768,768]{2,1,0:T(8,128)(2,1)}, ...) custom-call(s32[2]{0:T(128)} %bitcast.25, ...), custom_call_target="tpu_custom_call" | custom-call | tf_op jit(solution)/shard_map/front/pallas_call | solution.py:534
  93.6 104.5 %block_both.1 = (bf16[1536,768]{1,0:T(8,128)(2,1)}, f32[1536,768]{1,0:T(8,128)}, bf16[1536,768]{1,0:T(8,128)(2,1)}, bf16[768,768]{1,0:T(8,128)(2,1)}, bf16[768,3...) custom-call(bf16[6,1536,128]{2,1,0:T(8,128)(2,1)} %bitcast.21, f32[1536,768]{1,0:T(8,128)} %bitcast.14, ...), custom_call_target="tpu_custom_call" | custom-call | tf_op jit(solution)/shard_map/block_both/pallas_call | solution.py:718
  198.1 56.6 %attention_backward.1 = (bf16[2,768,768]{2,1,0:T(8,128)(2,1)}, bf16[2,768,768]{2,1,0:T(8,128)(2,1)}, bf16[2,768,768]{2,1,0:T(8,128)(2,1)}, f32[2,6,4,8,128]{4,3,...) custom-call(bf16[18,2,768,128]{3,2,1,0:T(8,128)(2,1)} %get-tuple-ele, ...), custom_call_target="tpu_custom_call" | custom-call | tf_op jit(solution)/shard_map/attention_backward/pallas_call | solution.py:1029
  254.7 69.2 %graph_backward.1 = (f32[2,768,768]{2,1,0:T(8,128)}, f32[2,768]{1,0:T(2,128)}, f32[3,768]{1,0:T(4,128)}, f32[3,768]{1,0:T(4,128)}, f32[24,1]{1,0:T(8,128)}, /*in...) custom-call(bf16[2,768,768]{2,1,0:T(8,128)(2,1)} %get-tuple-element., ...), custom_call_target="tpu_custom_call" | custom-call | tf_op jit(solution)/shard_map/graph_backward/pallas_call | solution.py:1323
  324.0 0.8 reduce
  324.8 0.1 reshape.81
  324.9 0.1 slice_reduce_fusion
  325.0 0.6 reshape_squeeze.7
  325.6 0.6 reshape_squeeze.6
  326.2 0.0 copy-start
  326.2 3.4 copy.47
  329.6 0.0 copy-done
  329.6 0.0 copy-start.8
  329.6 0.0 copy-start.7
  329.6 0.0 copy-start.6
  329.6 0.0 copy-start.5
  329.6 0.0 copy-start.11
  329.6 0.0 copy-start.3
  329.7 0.0 copy-start.4
  329.7 0.0 copy-start.2
  329.7 0.0 copy-start.1
  329.7 2.2 copy.48
  331.9 0.0 copy-done.8
  331.9 0.0 copy-start.10
  331.9 0.0 copy-start.9
  331.9 0.6 copy.49
  332.5 0.0 copy-done.7
  332.5 0.6 copy.50
  333.2 0.0 copy-done.6
  333.2 0.6 copy.51
  333.8 0.0 copy-done.5
  333.8 0.6 copy.52
  334.4 0.0 copy-done.11
  334.4 0.6 copy.53
  335.0 0.0 copy-done.3
  335.0 0.7 copy.54
  335.7 0.0 copy-done.4
  335.7 0.6 copy.55
  336.3 0.0 copy-done.2
  336.3 0.7 copy.56
  337.1 0.0 copy-done.1
  337.1 0.7 copy.57
  337.8 0.0 copy-done.10
  337.8 0.6 copy.58
  338.4 0.0 copy-done.9
  338.4 0.6 copy.59
Async XLA Ops:
  326.2 3.4 %copy-start = (f32[2,768,768]{2,1,0:T(8,128)S(1)}, f32[2,768,768]{2,1,0:T(8,128)}, u32[]{:S(2)}) copy-start(f32[2,768,768]{2,1,0:T(8,128)} %get-tuple-element.129) | copy-start | bytes 14155780
  329.6 2.3 copy-start.8
  329.6 2.9 copy-start.7
  329.6 3.5 %copy-start.6 = (f32[24,768]{1,0:T(8,128)S(1)}, f32[24,768]{1,0:T(8,128)}, u32[]{:S(2)}) copy-start(f32[24,768]{1,0:T(8,128)} %get-tuple-element.132) | copy-start | bytes 221188
  329.6 4.2 %copy-start.5 = (f32[24,768]{1,0:T(8,128)S(1)}, f32[24,768]{1,0:T(8,128)}, u32[]{:S(2)}) copy-start(f32[24,768]{1,0:T(8,128)} %get-tuple-element.133) | copy-start | bytes 221188
  329.6 4.8 %copy-start.11 = (f32[2,768]{1,0:T(2,128)S(1)}, f32[2,768]{1,0:T(2,128)}, u32[]{:S(2)}) copy-start(f32[2,768]{1,0:T(2,128)} %get-tuple-element.134) | copy-start | bytes 18436
  329.6 5.4 %copy-start.3 = (f32[24,2304]{1,0:T(8,128)S(1)}, f32[24,2304]{1,0:T(8,128)}, u32[]{:S(2)}) copy-start(f32[24,2304]{1,0:T(8,128)} %get-tuple-element.135) | copy-start | bytes 663556
  329.7 6.1 %copy-start.4 = (f32[24,768]{1,0:T(8,128)S(1)}, f32[24,768]{1,0:T(8,128)}, u32[]{:S(2)}) copy-start(f32[24,768]{1,0:T(8,128)} %get-tuple-element.136) | copy-start | bytes 221188
  329.7 6.7 %copy-start.2 = (f32[24,3072]{1,0:T(8,128)S(1)}, f32[24,3072]{1,0:T(8,128)}, u32[]{:S(2)}) copy-start(f32[24,3072]{1,0:T(8,128)} %get-tuple-element.137) | copy-start | bytes 884740
  329.7 7.4 %copy-start.1 = (f32[96,768]{1,0:T(8,128)S(1)}, f32[96,768]{1,0:T(8,128)}, u32[]{:S(2)}) copy-start(f32[96,768]{1,0:T(8,128)} %get-tuple-element.138) | copy-start | bytes 884740
  331.9 5.9 %copy-start.10 = (f32[3,768]{1,0:T(4,128)S(1)}, f32[3,768]{1,0:T(4,128)}, u32[]{:S(2)}) copy-start(f32[3,768]{1,0:T(4,128)} %get-tuple-element.139) | copy-start | bytes 27652
  331.9 6.5 %copy-start.9 = (f32[3,768]{1,0:T(4,128)S(1)}, f32[3,768]{1,0:T(4,128)}, u32[]{:S(2)}) copy-start(f32[3,768]{1,0:T(4,128)} %get-tuple-element.140) | copy-start | bytes 27652
